TPU v7x, 32 devices: a whole 2x2x4 slice. The times are simulated.
32 devices in a mesh: groups: 2 (over x), wide: 16 (over z, y, core).
Axes of the slice: x: 2, y: 2, z: 4, core: 2. Of those that a mesh axis runs over, the one named last changes fastest.
Arguments:
- fine_field: float32 [256, 64, 512], P(None, ('groups', 'wide')), parts along dimension 1, may hold values from -6 to 6
- w_down_fine: float32 [8, 256, 512], replicated, may hold values from -0.125 to 0.125
- w_conv_mid: float32 [27, 512, 512], P(None, 'wide'), may hold values from -0.0546875 to 0.0546875
- w_down_mid: float32 [8, 512, 1024], P(None, 'wide'), may hold values from -0.09375 to 0.09375
- w_conv_deep: float32 [27, 1024, 1024], P(None, 'wide'), may hold values from -0.0390625 to 0.0390625
- w_up_deep: float32 [8, 1024, 512], P(None, 'wide'), may hold values from -0.1875 to 0.1875
- w_up_mid: float32 [8, 512, 256], replicated, may hold values from -0.25 to 0.25
Outputs:
- fine_update: float32 [256, 64, 512], P(None, ('groups', 'wide')), parts along dimension 1
There are 2 independent parts, one for each index of `groups`. A program takes and returns all parts, laid end to end along the dimension named above; an argument that names none is the same for every part. Nothing has to cross between parts.
All inputs are finite; a program needn't handle non-finite values.
Results may differ from a plain program's by a relative error of at most 0.0001.
Values sent between devices are 32-bit elements; how exact they have to be, the bound alone decides.
A program may use at most 192 MiB of HBM per device.

v0:
```python
import jax
import jax.numpy as jnp
from jax import lax
from jax.sharding import PartitionSpec as P

YA = 32
ZA = 16


HIGHEST_MODE = lax.Precision.HIGHEST


def selector(rows, cols, b, c):
    big_cells = jnp.arange(rows * cols)[:, None]
    small_cells = jnp.arange(rows // 2 * (cols // 2))[None, :]
    target = (2 * (small_cells // (cols // 2)) + b) * cols + 2 * (small_cells % (cols // 2)) + c
    return (big_cells == target).astype(jnp.float32)


def valid_mask(cells, rows, cols, step_row, step_col):
    places = jnp.arange(cells)
    row_of = places // cols % rows + step_row
    col_of = places % cols + step_col
    inside = (row_of >= 0) & (row_of < rows) & (col_of >= 0) & (col_of < cols)
    return inside.astype(jnp.float32)


def shift_flat(field, offset, weights_mask):
    width = abs(offset)
    last = field.ndim - 1
    padded = jnp.pad(field, [(0, 0)] * last + [(width, width)])
    cells = field.shape[last]
    shifted = lax.slice_in_dim(padded, width + offset, width + offset + cells, axis=last)
    return shifted * weights_mask


def lift_apply(weights, source, row_count, mid_rows, mid_cols, deep_planes, deep_rows, deep_cols):
    mid_planes = 2 * deep_planes
    mid_cells = mid_rows * mid_cols
    spread = jnp.einsum("tco,cn->ton", weights, source, precision=HIGHEST_MODE)
    summed = jnp.zeros((2, row_count, deep_planes, mid_cells), jnp.float32)
    for b in range(2):
        for c in range(2):
            paired = jnp.stack([spread[2 * b + c], spread[4 + 2 * b + c]])
            paired = paired.reshape(2, row_count, deep_planes, deep_rows * deep_cols)
            summed = summed + jnp.dot(
                paired, selector(mid_rows, mid_cols, b, c).T, precision=HIGHEST_MODE
            )
    return summed.transpose(1, 2, 0, 3).reshape(row_count, mid_planes, mid_cells)


def shards(fine_field, w_down_fine, w_conv_mid, w_down_mid, w_conv_deep, w_up_deep, w_up_mid):
    wide_count = lax.axis_size("wide")
    mid_rows, mid_cols = (YA // 2, ZA // 2)
    deep_rows, deep_cols = (YA // 4, ZA // 4)
    mid_cells = mid_rows * mid_cols
    deep_planes = wide_count // 2
    deep_cells = deep_planes * deep_rows * deep_cols
    chan_fine = fine_field.shape[0]
    chan_mid = w_down_fine.shape[2]
    chan_deep = w_down_mid.shape[2]
    mid_local = w_conv_mid.shape[1]
    deep_local = w_conv_deep.shape[1]
    fine_picks = [None] * 8
    for b in range(2):
        for c in range(2):
            reduced = jnp.dot(fine_field, selector(YA, ZA, b, c), precision=HIGHEST_MODE)
            for a in range(2):
                fine_picks[4 * a + 2 * b + c] = reduced[:, a, :]
    mid_input = jnp.einsum(
        "tco,tcn->on", w_down_fine, jnp.stack(fine_picks), precision=HIGHEST_MODE
    )[:, None, :]
    mid_kernel = w_conv_mid.reshape(3, 3, 3, mid_local, chan_mid)
    mid_start = jnp.zeros((mid_local, wide_count + 2, mid_cells), jnp.float32)
    running = mid_start
    shard_piece = lax.all_gather(mid_input, "wide", axis=1, tiled=True)
    first_row = jnp.int32(0)
    row_count = shard_piece.shape[1]
    summed = jnp.zeros((3, mid_local, row_count, mid_cells), jnp.float32)
    for convolve_b in range(3):
        for convolve_c in range(3):
            shifted = shift_flat(
                shard_piece,
                (convolve_b - 1) * mid_cols + (convolve_c - 1),
                valid_mask(mid_cells, mid_rows, mid_cols, convolve_b - 1, convolve_c - 1),
            )
            summed = summed + jnp.einsum(
                "aoc,ckn->aokn",
                mid_kernel[:, convolve_b, convolve_c],
                shifted,
                precision=HIGHEST_MODE,
            )
    for convolve_a in range(3):
        offset_row = first_row - convolve_a + 2
        current = lax.dynamic_slice_in_dim(running, offset_row, row_count, 1)
        running = lax.dynamic_update_slice_in_dim(
            running, current + summed[convolve_a], offset_row, 1
        )
    folded = running
    mid_field = jax.nn.relu(folded[:, 1:-1])
    deep_picks = [None] * 8
    for b in range(2):
        for c in range(2):
            reduced = jnp.dot(mid_field, selector(mid_rows, mid_cols, b, c), precision=HIGHEST_MODE)
            reduced = reduced.reshape(mid_local, deep_planes, 2, deep_rows * deep_cols)
            for a in range(2):
                deep_picks[4 * a + 2 * b + c] = reduced[:, :, a, :].reshape(mid_local, deep_cells)
    deep_stack = jnp.stack(deep_picks)
    deep_kernel = w_conv_deep.reshape(3, 3, 3, deep_local, chan_deep)

    def convolve_deep(running, shard_piece):
        row_count = shard_piece.shape[0]
        for a in range(3):
            shifted_list = []
            for b in range(3):
                for c in range(3):
                    offset = (a - 1) * deep_rows * deep_cols + (b - 1) * deep_cols + (c - 1)
                    shifted_list.append(
                        shift_flat(
                            shard_piece,
                            offset,
                            valid_mask(deep_cells, deep_rows, deep_cols, b - 1, c - 1),
                        )
                    )
            shifted = jnp.stack(shifted_list)
            running = running + jnp.einsum(
                "tok,tkn->on",
                deep_kernel[a].reshape(9, deep_local, row_count),
                shifted,
                precision=HIGHEST_MODE,
            )
        return running

    deep_start = jnp.zeros((deep_local, deep_cells), jnp.float32)
    deep_part = jax.nn.relu(
        lax.psum_scatter(
            jnp.einsum("tco,tcn->on", w_down_mid, deep_stack, precision=HIGHEST_MODE),
            "wide",
            scatter_dimension=0,
            tiled=True,
        )
    )
    deep_output = jax.nn.relu(
        convolve_deep(deep_start, lax.all_gather(deep_part, "wide", axis=0, tiled=True))
    )
    deep_every = lax.all_gather(deep_output, "wide", axis=0, tiled=True)
    w_columns = lax.all_to_all(w_up_deep, "wide", split_axis=2, concat_axis=1, tiled=True)
    lifted = lift_apply(
        w_columns, deep_every, mid_local, mid_rows, mid_cols, deep_planes, deep_rows, deep_cols
    )
    mid_merged = jax.nn.relu(mid_field + lifted)
    merged_every = lax.all_gather(mid_merged, "wide", axis=0, tiled=True)
    mid_plane = lax.dynamic_slice_in_dim(merged_every, lax.axis_index("wide"), 1, 1)
    spread_fine = jnp.einsum("tco,cn->ton", w_up_mid, mid_plane[:, 0, :], precision=HIGHEST_MODE)
    fine_sum = jnp.zeros((2, chan_fine, YA * ZA), jnp.float32)
    for b in range(2):
        for c in range(2):
            paired = jnp.stack([spread_fine[2 * b + c], spread_fine[4 + 2 * b + c]])
            fine_sum = fine_sum + jnp.dot(paired, selector(YA, ZA, b, c).T, precision=HIGHEST_MODE)
    return fine_sum.transpose(1, 0, 2)


def solution(mesh):
    return jax.shard_map(
        shards,
        mesh=mesh,
        in_specs=(
            P(None, ("groups", "wide"), None),
            P(),
            P(None, "wide", None),
            P(None, "wide", None),
            P(None, "wide", None),
            P(None, "wide", None),
            P(),
        ),
        out_specs=P(None, ("groups", "wide"), None),
        check_vma=False,
    )
```

profile of v0, /device:TPU:0, one launch (start us, length us, event | category | flops | bytes accessed | tf_op | source)
XLA Modules:
  0.0 358.2 jit_solution(16231777582741179263)
XLA Ops:
  11.1 3.1 convolution_bitcast_fusion.2
  14.5 53.2 %all-gather.12.cloned.1.call-done = f32[512,2048]{0,1:T(8,128)} async-done(((f32[512,128]{0,1:T(8,128)}), f32[512,2048]{0,1:T(8,128)}) %all-gather.12.cloned.1.call-update) | async-done | bytes 4194320 | tf_op jit(solution)/shard_map/all_gather | solution.py:76
  67.7 5.6 %copy.118 = f32[512,16,128]{2,0,1:T(8,128)} copy(f32[512,16,128]{0,2,1:T(8,128)} %bitcast.430) | data formatting | bytes 8388608 | tf_op jit(solution)/shard_map/all_gather | solution.py:76
  73.4 5.4 %fusion.2 = f32[16,128,3,32]{1,3,2,0:T(8,128)S(1)} fusion(f32[512,16,128]{2,0,1:T(8,128)} %copy.118, f32[128]{0:T(128)S(1)} %and_convert_fusion.17, f32[3,3,3,32,512]{4,3,2,1,0:T(8,128)S(1)} %bitcast.431), kind=kOutput, calls=%fused_computation.10 | convolution fusion | flops 1209008128 | bytes 5177856 | tf_op jit(solution)/shard_map/aoc,ckn->aokn/dot_general | solution.py:87
  78.8 2.8 fusion.32
  81.6 3.1 fusion.66
  84.6 3.1 fusion.60
  87.7 3.3 fusion.75
  91.0 3.1 fusion.51
  94.0 3.1 fusion.57
  97.1 3.1 fusion.63
  100.1 3.5 fusion.72
  104.6 1.5 slice_reduce_fusion
  107.0 1.5 slice_reduce_fusion.2
  109.3 2.3 convolution_bitcast_fusion.1
  112.9 56.0 %reduce-scatter.4.cloned.1.call-done = f32[64,256]{1,0:T(8,128)} async-done(((f32[1024,256]{1,0:T(8,128)}), f32[64,256]{1,0:T(8,128)}) %reduce-scatter.4.cloned.1.call-update) | async-done | bytes 65552 | tf_op jit(solution)/shard_map/reduce_scatter | solution.py:136
  168.9 1.5 broadcast_maximum_fusion
  171.2 2.3 reshape.464
  173.4 3.7 %all-to-all-start = ((f32[16,1,16384]{2,1,0:T(1,128)}), f32[16,1,16384]{2,1,0:T(1,128)S(1)}, u32[]{:S(2)}, u32[]{:S(2)}) async-start(f32[16,1,16384]{2,1,0:T(1,128)} %reshape.464), calls=%async_computation | async-start | bytes 2097152 | tf_op jit(solution)/shard_map/all_to_all | solution.py:147
  177.5 40.5 %all-gather.6.cloned.1.call-done = f32[1024,256]{1,0:T(8,128)} async-done(((f32[64,256]{1,0:T(8,128)}), f32[1024,256]{1,0:T(8,128)}) %all-gather.6.cloned.1.call-update) | async-done | bytes 1048592 | tf_op jit(solution)/shard_map/all_gather | solution.py:144
  218.0 3.0 fusion.102
  227.7 7.3 %fusion.94 = f32[256,64]{0,1:T(8,128)S(1)} fusion(f32[9,1024,256]{2,1,0:T(8,128)S(1)} %get-tuple-element.15, f32[27,64,1024]{2,1,0:T(8,128)} %param.11), kind=kOutput, calls=%fused_computation.105 | convolution fusion | flops 1811939328 | bytes 11862016 | tf_op jit(solution)/shard_map/tok,tkn->on/dot_general | solution.py:126
  235.0 7.5 %fusion.97 = f32[256,64]{0,1:T(8,128)S(1)} fusion(f32[9,1024,256]{2,1,0:T(8,128)S(1)} %get-tuple-element.14, f32[27,64,1024]{2,1,0:T(8,128)} %param.11), kind=kOutput, calls=%fused_computation.106 | convolution fusion | flops 1811939328 | bytes 11862016 | tf_op jit(solution)/shard_map/tok,tkn->on/dot_general | solution.py:126
  242.6 7.9 %fusion.91 = f32[64,256]{1,0:T(8,128)} fusion(f32[256,64]{0,1:T(8,128)S(1)} %fusion.97, f32[256,64]{0,1:T(8,128)S(1)} %fusion.94, f32[9,1024,256]{2,1,0:T(8,128)S(1)} %get-tuple-element.13, f32[27,64,1024]{2,1,0:T(8,128)} %param.11), kind=kOutput, calls=%fused_computation.104 | convolution fusion | flops 1811988480 | bytes 11993088 | tf_op jit(solution)/shard_map/tok,tkn->on/dot_general | solution.py:126
  251.3 3.2 reduce.32
  255.3 2.5 copy.141
  257.9 2.0 all_to_all.16
  259.9 27.6 %all-gather.8.cloned.1.call-done = f32[1024,256]{1,0:T(8,128)} async-done(((f32[64,256]{1,0:T(8,128)}), f32[1024,256]{1,0:T(8,128)}) %all-gather.8.cloned.1.call-update) | async-done | bytes 1048592 | tf_op jit(solution)/shard_map/all_gather | solution.py:146
  287.5 2.3 fusion.287
  292.5 49.6 %all-gather.10.cloned.1.call-done = f32[512,16,128]{2,0,1:T(8,128)} async-done(((f32[32,16,128]{2,0,1:T(8,128)}), f32[512,16,128]{2,0,1:T(8,128)}) %all-gather.10.cloned.1.call-update) | async-done | bytes 4194320 | tf_op jit(solution)/shard_map/all_gather | solution.py:152
  342.2 4.6 %convolution_bitcast_fusion = f32[8,256,128]{1,2,0:T(8,128)S(1)} fusion(f32[8,512,256]{2,1,0:T(8,128)} %param.13, f32[512,16,128]{2,0,1:T(8,128)} %all-gather.10.cloned.1.call-done, s32[]{:T(128)S(6)} %select_n.760), kind=kOutput, calls=%fused_computation.76 | convolution fusion | flops 1610612736 | bytes 5505028 | tf_op jit(solution)/shard_map/tco,cn->ton/dot_general | solution.py:154
  349.4 1.8 copy.148
  (116 shorter events, 23.3 us)
Async XLA Ops:
  6.5 1.2 copy-start
  6.5 61.2 %all-gather.12.cloned.1.call-start = ((), (), s32[]{:S(2)}) async-start(), calls=%async_computation.5 | async-start | bytes 4456448 | tf_op jit(solution)/shard_map/all_gather | solution.py:76
  6.5 4.6 %copy-start.4 = (f32[8,256,512]{2,1,0:T(8,128)S(1)}, f32[8,256,512]{2,1,0:T(8,128)}, u32[]{:S(2)}) copy-start(f32[8,256,512]{2,1,0:T(8,128)} %param.8) | copy-start | bytes 12582916
  14.3 154.6 %reduce-scatter.4.cloned.1.call-start = ((), (), s32[]{:S(2)}) async-start(), calls=%async_computation.6 | async-start | bytes 1114112 | tf_op jit(solution)/shard_map/reduce_scatter | solution.py:136
  67.7 5.7 %copy-start.5 = (f32[27,32,512]{2,1,0:T(8,128)S(1)}, f32[27,32,512]{2,1,0:T(8,128)}, u32[]{:S(2)}) copy-start(f32[27,32,512]{2,1,0:T(8,128)} %param.9) | copy-start | bytes 5308420
  73.3 5.4 %copy-start.2 = (f32[512,16,128]{2,0,1:T(8,128)S(1)}, f32[512,16,128]{2,0,1:T(8,128)}, u32[]{:S(2)}) copy-start(f32[512,16,128]{2,0,1:T(8,128)} %copy.118) | copy-start | bytes 12582916
  108.6 61.8 %copy-start.6 = (f32[8,64,512]{2,1,0:T(8,128)S(1)}, f32[8,64,512]{2,1,0:T(8,128)}, u32[]{:S(2)}) copy-start(f32[8,64,512]{2,1,0:T(8,128)} %param.12) | copy-start | bytes 3145732
  112.9 105.1 %all-gather.6.cloned.1.call-start = ((), (), s32[]{:S(2)}) async-start(), calls=%async_computation.2 | async-start | bytes 1114112 | tf_op jit(solution)/shard_map/all_gather | solution.py:144
  173.4 77.4 %all-to-all-start = ((f32[16,1,16384]{2,1,0:T(1,128)}), f32[16,1,16384]{2,1,0:T(1,128)S(1)}, u32[]{:S(2)}, u32[]{:S(2)}) async-start(f32[16,1,16384]{2,1,0:T(1,128)} %reshape.464), calls=%async_computation | async-start | bytes 2097152 | tf_op jit(solution)/shard_map/all_to_all | solution.py:147
  177.2 110.3 %all-gather.8.cloned.1.call-start = ((), (), s32[]{:S(2)}) async-start(), calls=%async_computation.3 | async-start | bytes 1114112 | tf_op jit(solution)/shard_map/all_gather | solution.py:146
  218.0 3.0 copy-start.3
  250.5 91.7 %all-gather.10.cloned.1.call-start = ((), (), s32[]{:S(2)}) async-start(), calls=%async_computation.4 | async-start | bytes 4456448 | tf_op jit(solution)/shard_map/all_gather | solution.py:152
  347.5 3.7 %copy-start.1 = (f32[256,2,512]{2,1,0:T(2,128)S(1)}, f32[256,2,512]{2,1,0:T(2,128)}, u32[]{:S(2)}) copy-start(f32[256,2,512]{2,1,0:T(2,128)} %param.7) | copy-start | bytes 3145732
Sparse Core Ops, SparseCore 0:
  14.4 53.2 all-gather.11
  113.0 55.8 reduce-scatter.3
  171.3 46.6 all-gather.5
  250.6 36.8 all-gather.7
  292.6 49.4 all-gather.9
where the time goes:
time: 363 us; the launch traced here: 358 us
  waiting for transfers between devices  227 us (63%)
  matrix products  73.8 us (20%)
  local copies, waits for them, and re-layouts  23.3 us (6%)
  other arithmetic  15.5 us (4%)
  between operations  14.3 us (4%)
  starting transfers between devices  4.33 us (1%)
    reduce_scatter x1, waiting for transfers between devices, shards(): lax.psum_scatter(jnp.einsum('tco,tcn->on', w_down_mid, deep_stack, precis...  56 us
    all_gather x1, waiting for transfers between devices, shards(): shard_piece = lax.all_gather(mid_input, 'wide', axis=1, tiled=True)  53.2 us
    all_gather x1, waiting for transfers between devices, shards(): merged_every = lax.all_gather(mid_merged, 'wide', axis=0, tiled=True)  49.6 us
    all_gather x1, waiting for transfers between devices, shards(): lax.all_gather(deep_part, 'wide', axis=0, tiled=True)  40.5 us
    dot_general x9, matrix products, shards(): jnp.einsum('aoc,ckn->aokn', mid_kernel[:, convolve_b, convolve_c], shifte...  30.2 us
    all_gather x1, waiting for transfers between devices, shards(): deep_every = lax.all_gather(deep_output, 'wide', axis=0, tiled=True)  27.6 us
    dot_general x3, matrix products, convolve_deep(): jnp.einsum('tok,tkn->on', deep_kernel[a].reshape(9, deep_local, row_count...  22.7 us
    unnamed x8, other arithmetic  8.85 us
  transfers between devices with their start and end apart: 6, of which 5 were waited for; matrix products, arithmetic and copies ran while one was open for 12% of the time, Pallas kernels for 0%

commit v1 on v0

v1 whole, which is shorter than its diff:
```python
import functools

import jax
import jax.numpy as jnp
from jax import lax
from jax.experimental import pallas as pl
from jax.experimental.pallas import tpu as pltpu
from jax.sharding import PartitionSpec as P

YA = 32
ZA = 16
MESH = pl.DeviceIdType.MESH
BF16 = jnp.bfloat16
F32 = jnp.float32


def selector(rows, cols, copies):
    cells = rows * cols
    small = cells // 4
    source = jnp.arange(copies * cells)[:, None]
    target = jnp.arange(4 * copies * small)[None, :]
    tap = target // (copies * small)
    copy = target // small % copies
    place = target % small
    row = 2 * (place // (cols // 2)) + tap // 2
    col = 2 * (place % (cols // 2)) + tap % 2
    return (source == copy * cells + row * cols + col).astype(F32)


def split(value):
    high = value.astype(BF16)
    return high, (value - high.astype(F32)).astype(BF16)


def dot(left, right):
    return lax.dot_general(left, right, (((1,), (0,)), ((), ())), preferred_element_type=F32)


def dot_nt(left, right):
    return lax.dot_general(left, right, (((1,), (1,)), ((), ())), preferred_element_type=F32)


def dot3(left_high, left_low, right_high, right_low):
    return dot(left_high, right_high) + dot(left_high, right_low) + dot(left_low, right_high)


def middle_kernel(
    wide, groups,
    mid_in, w_mid, w_down, w_deep_hbm, w_up, sel, out,
    xbuf, xh, xl, wmh, wml, acc, mf, wdh, wdl, part, sib, rs, rsin,
    deep_in, wdeep, wch, wcl, deep_out, wup, wuh, wul, mm, landed,
    s1, r1, s2, r2, s3, r3, s_sib, r_sib, s_rs, r_rs, s_up, r_up, s_fw, r_fw, s_aa, r_aa, load_sem,
):
    ny = 2 if wide % 4 == 0 else 1
    nchip = wide // 2
    nz = nchip // ny
    me = lax.axis_index("wide")
    mygroup = lax.axis_index("groups")
    core = me % 2
    chip = me // 2
    y = chip % ny
    z = chip // ny
    mid_local = mf.shape[1]
    cells = mf.shape[2]
    rows, cols = YA // 2, ZA // 2
    drows, dcols = YA // 4, ZA // 4
    dcells = drows * dcols
    deep_local = deep_in.shape[1]
    dn = deep_in.shape[2]
    ngr = dn // cells

    load = pltpu.make_async_copy(w_deep_hbm, wdeep, load_sem)
    load.start()

    barrier = pltpu.get_barrier_semaphore()
    for step in range(1, wide):
        pl.semaphore_signal(barrier, inc=1, device_id={"wide": (me + step) % wide}, device_id_type=MESH)
    for step in range(1, groups):
        pl.semaphore_signal(barrier, inc=1, device_id={"groups": (mygroup + step) % groups}, device_id_type=MESH)
    pl.semaphore_wait(barrier, wide + groups - 2)

    def slot(zz, yy, cc):
        return (zz * ny + yy) * 2 + cc

    def gather(buf, send_sem, recv_sem, consume, idle):
        def move(at, target, k):
            return pltpu.make_async_remote_copy(
                src_ref=buf.at[at], dst_ref=buf.at[at], send_sem=send_sem.at[k], recv_sem=recv_sem.at[at],
                device_id={"wide": target}, device_id_type=MESH)

        def arrived(at):
            move(at, slot(z, y, 1 - core), 0).wait_recv()

        sibling = slot(z, y, 1 - core)
        other = slot(z, ny - 1 - y, core)
        if ny == 2:
            move(me, other, nz).start()
        move(me, sibling, 2 * nz).start()
        for dz in range(1, nz):
            move(me, slot((z + nz - dz) % nz, y, core), dz - 1).start()
        idle()
        arrived(sibling)
        consume(chip)

        def other_row(dz):
            zp = (z + dz) % nz
            at = slot(zp, 1 - y, core)
            arrived(at)
            move(at, sibling, 2 * nz + dz * ny + 1).start()

        def step(dz, carry):
            zs = (z + dz) % nz
            at = slot(zs, y, core)
            arrived(at)
            if ny == 2:
                move(at, other, nz + dz).start()
            move(at, sibling, 2 * nz + dz * ny).start()
            if ny == 2:
                other_row(dz - 1)
            arrived(slot(zs, y, 1 - core))
            consume(zs * ny + y)
            if ny == 2:
                zp = (z + dz - 1) % nz
                arrived(slot(zp, 1 - y, 1 - core))
                consume(zp * ny + 1 - y)
            return carry

        lax.fori_loop(1, nz, step, 0)
        if ny == 2:
            other_row(nz - 1)
            zp = (z + nz - 1) % nz
            arrived(slot(zp, 1 - y, 1 - core))
            consume(zp * ny + 1 - y)

        def finish():
            for k in range(nz - 1):
                move(me, sibling, k).wait_send()
            if ny == 2:
                for k in range(nz):
                    move(me, sibling, nz + k).wait_send()
            for k in range(nz * ny):
                move(me, sibling, 2 * nz + k).wait_send()

        return finish

    xbuf[me] = mid_in[...]
    taps = 9 * mid_local
    lane = lax.broadcasted_iota(jnp.int32, (mid_local, cells), 1)
    mid_masks = {}
    for b in range(3):
        for c in range(3):
            r, s = lane // cols + b - 1, lane % cols + c - 1
            mid_masks[b, c] = (r >= 0) & (r < rows) & (s >= 0) & (s < cols)

    def convolve_mid(at):
        for h in range(2):
            high, low = split(xbuf[at * 2 + h])
            xh[:, h * cells:(h + 1) * cells] = high
            xl[:, h * cells:(h + 1) * cells] = low

        def plane_tap(a, carry):
            here = pl.ds(pl.multiple_of(a * taps, taps), taps)
            product = dot3(wmh[here, :], wml[here, :], xh[...], xl[...])
            for h in range(2):
                total = jnp.zeros((mid_local, cells), F32)
                for b in range(3):
                    for c in range(3):
                        tap = 3 * b + c
                        piece = product[tap * mid_local:(tap + 1) * mid_local, h * cells:(h + 1) * cells]
                        offset = (b - 1) * cols + c - 1
                        if offset:
                            piece = pltpu.roll(piece, (-offset) % cells, 1)
                            piece = jnp.where(mid_masks[b, c], piece, 0.0)
                        total = total + piece
                acc[at * 2 + h - a + 2] += total
            return carry

        lax.fori_loop(0, 3, plane_tap, 0)

    def prepare_mid():
        acc[...] = jnp.zeros_like(acc)
        wmh[...], wml[...] = split(w_mid[...])
        wdh[...], wdl[...] = split(w_down[...].T)

    finish_mid = gather(xbuf, s1, r1, convolve_mid, prepare_mid)

    share = wup.shape[1] // groups
    mine = pl.ds(pl.multiple_of(mygroup * share, share), share)

    def up_move(target, source):
        return pltpu.make_async_remote_copy(
            src_ref=w_up.at[target, mine], dst_ref=wup.at[me, mine], send_sem=s_up.at[target], recv_sem=r_up.at[source],
            device_id={"wide": target}, device_id_type=MESH)

    def up_arrived(source):
        pltpu.make_async_remote_copy(
            src_ref=w_up.at[source, mine], dst_ref=wup.at[source, mine], send_sem=s_up.at[source], recv_sem=r_up.at[source],
            device_id={"wide": source}, device_id_type=MESH).wait_recv()

    mf[...] = jnp.maximum(acc[1:wide + 1], 0.0)

    gathered = []
    for a in range(2):
        for g in range(ngr):
            gathered.append(jnp.concatenate([mf[2 * (4 * g + p) + a] for p in range(4)], axis=1))
    high, low = split(jnp.concatenate(gathered, axis=0))
    high, low = dot(high, sel[...]).astype(BF16), dot(low, sel[...]).astype(BF16)

    def spread_rows(value):
        blocks = []
        for a in range(2):
            for bc in range(4):
                blocks.append(jnp.concatenate([
                    value[(a * ngr + g) * mid_local:(a * ngr + g + 1) * mid_local, bc * cells:(bc + 1) * cells]
                    for g in range(ngr)], axis=1))
        return jnp.concatenate(blocks, axis=0)

    high, low = spread_rows(high), spread_rows(low)
    part[...] = dot3(wdh[...], wdl[...], high, low).reshape(part.shape)
    sibling_id = chip * 2 + 1 - core
    pair = pltpu.make_async_remote_copy(
        src_ref=part.at[:, 1 - core], dst_ref=sib, send_sem=s_sib, recv_sem=r_sib,
        device_id={"wide": sibling_id}, device_id_type=MESH)
    pair.start()

    load.wait()

    def split_deep(t, carry):
        here = pl.ds(pl.multiple_of(t * deep_local, deep_local), deep_local)
        wch[here, :], wcl[here, :] = split(wdeep[here, :])
        return carry

    pair.wait_recv()

    def rs_move(target, source, k):
        return pltpu.make_async_remote_copy(
            src_ref=rs.at[target], dst_ref=rsin.at[source], send_sem=s_rs.at[k], recv_sem=r_rs.at[source],
            device_id={"wide": target * 2 + core}, device_id_type=MESH)

    for step in range(1, nchip):
        target = (chip + step) % nchip
        rs[target] = part[target, core] + sib[target]
        rs_move(target, chip, step).start()
    for step in range(1, wide):
        target = (me + step) % wide
        up_move(target, me).start()
    wup[me, mine] = w_up[me, mine]
    lax.fori_loop(0, 27, split_deep, 0)
    total = part[chip, core] + sib[chip]
    for step in range(1, nchip):
        source = (chip + nchip - step) % nchip
        rs_move(source, source, step).wait_recv()
        total = total + rsin[source]
    deep_in[me] = jnp.maximum(total, 0.0)

    def nothing(*args):
        return None

    finish_in = gather(deep_in, s2, r2, nothing, nothing)
    for step in range(1, wide):
        up_arrived((me + wide - step) % wide)

    def forward(target, source):
        return pltpu.make_async_remote_copy(
            src_ref=wup.at[:, mine], dst_ref=wup.at[:, mine], send_sem=s_fw.at[target], recv_sem=r_fw.at[mygroup],
            device_id={"groups": target}, device_id_type=MESH)

    for step in range(1, groups):
        forward((mygroup + step) % groups, mygroup).start()

    dh, dl = split(deep_in[...].reshape(wide * deep_local, dn))
    dlane = lax.broadcasted_iota(jnp.int32, (deep_local, dn), 1)
    total = jnp.zeros((deep_local, dn), F32)
    for a in range(3):
        here = slice(a * 9 * deep_local, (a + 1) * 9 * deep_local)
        product = dot3(wch[here, :], wcl[here, :], dh, dl)
        for b in range(3):
            for c in range(3):
                tap = 3 * b + c
                piece = product[tap * deep_local:(tap + 1) * deep_local]
                offset = (a - 1) * dcells + (b - 1) * dcols + c - 1
                if offset:
                    piece = pltpu.roll(piece, (-offset) % dn, 1)
                    p, r, s = dlane // dcells + a - 1, dlane // dcols % drows + b - 1, dlane % dcols + c - 1
                    inside = (p >= 0) & (p < dn // dcells) & (r >= 0) & (r < drows) & (s >= 0) & (s < dcols)
                    piece = jnp.where(inside, piece, 0.0)
                total = total + piece
    deep_out[me] = jnp.maximum(total, 0.0)

    def prepare_up():
        for step in range(1, groups):
            source = (mygroup + groups - step) % groups
            theirs = pl.ds(pl.multiple_of(source * share, share), share)
            pltpu.make_async_remote_copy(
                src_ref=wup.at[:, theirs], dst_ref=wup.at[:, theirs], send_sem=s_fw.at[source],
                recv_sem=r_fw.at[source], device_id={"groups": source}, device_id_type=MESH).wait_recv()
        wuh[...], wul[...] = split(wup[...].reshape(wide * deep_local, wup.shape[2]).T)

    finish_out = gather(deep_out, s3, r3, nothing, prepare_up)
    dh, dl = split(deep_out[...].reshape(wide * deep_local, dn))
    lifted = dot3(wuh[...], wul[...], dh, dl)
    blocks = []
    for a in range(2):
        for g in range(ngr):
            blocks.append(jnp.concatenate([
                lifted[(a * 4 + bc) * mid_local:(a * 4 + bc + 1) * mid_local, g * cells:(g + 1) * cells]
                for bc in range(4)], axis=1))
    high, low = split(jnp.concatenate(blocks, axis=0))
    spread = dot_nt(high, sel[...]) + dot_nt(low, sel[...])
    for a in range(2):
        for g in range(ngr):
            for p in range(4):
                plane = 2 * (4 * g + p) + a
                block = spread[(a * ngr + g) * mid_local:(a * ngr + g + 1) * mid_local, p * cells:(p + 1) * cells]
                mm[plane] = jnp.maximum(mf[plane] + block, 0.0)

    def plane_move(target, source):
        return pltpu.make_async_remote_copy(
            src_ref=mm.at[target], dst_ref=landed.at[source], send_sem=s_aa.at[target], recv_sem=r_aa.at[source],
            device_id={"wide": target}, device_id_type=MESH)

    for step in range(1, wide):
        plane_move((me + step) % wide, me).start()
    landed[me] = mm[me]
    finish_mid()
    finish_in()
    finish_out()
    pair.wait_send()
    for step in range(1, nchip):
        rs_move((chip + step) % nchip, chip, step).wait_send()
    for step in range(1, wide):
        up_move((me + step) % wide, me).wait_send()
    for step in range(1, groups):
        forward((mygroup + step) % groups, mygroup).wait_send()
    for step in range(1, wide):
        plane_move((me + step) % wide, me).wait_send()
    for step in range(1, wide):
        source = (me + wide - step) % wide
        plane_move(source, source).wait_recv()
    out[...] = landed[...]


def shards(wide, groups, fine_field, w_down_fine, w_conv_mid, w_down_mid, w_conv_deep, w_up_deep, w_up_mid):
    chan_fine = fine_field.shape[0]
    chan_mid = w_down_fine.shape[2]
    chan_deep = w_down_mid.shape[2]
    mid_local = w_conv_mid.shape[1]
    deep_local = w_conv_deep.shape[1]
    cells = YA // 2 * (ZA // 2)
    dn = wide // 2 * (cells // 4)
    nchip = wide // 2
    high = lax.Precision.HIGH

    fine_sel = selector(YA, ZA, 1)
    picks = jnp.dot(fine_field.reshape(chan_fine * 2, YA * ZA), fine_sel, precision=high)
    picks = picks.reshape(chan_fine, 2, 4, cells).transpose(1, 2, 0, 3).reshape(8 * chan_fine, cells)
    mid_input = lax.dot_general(
        w_down_fine.reshape(8 * chan_fine, chan_mid), picks, (((0,), (0,)), ((), ())), precision=high)
    up_blocks = w_up_deep.reshape(8, deep_local, wide, mid_local).transpose(2, 1, 0, 3)
    up_blocks = up_blocks.reshape(wide, deep_local, 8 * mid_local)
    sel = selector(YA // 2, ZA // 2, 4).astype(BF16)

    vmem = pl.BlockSpec(memory_space=pltpu.VMEM)
    dma = pltpu.SemaphoreType.DMA
    sends = 4 * nchip
    merged = pl.pallas_call(
        functools.partial(middle_kernel, wide, groups),
        out_shape=jax.ShapeDtypeStruct((wide, mid_local, cells), F32),
        in_specs=[vmem, vmem, vmem, pl.BlockSpec(memory_space=pl.ANY), vmem, vmem],
        out_specs=vmem,
        scratch_shapes=[
            pltpu.VMEM((wide, chan_mid, cells), F32),
            pltpu.VMEM((chan_mid, 2 * cells), BF16),
            pltpu.VMEM((chan_mid, 2 * cells), BF16),
            pltpu.VMEM((27 * mid_local, chan_mid), BF16),
            pltpu.VMEM((27 * mid_local, chan_mid), BF16),
            pltpu.VMEM((wide + 2, mid_local, cells), F32),
            pltpu.VMEM((wide, mid_local, cells), F32),
            pltpu.VMEM((chan_deep, 8 * mid_local), BF16),
            pltpu.VMEM((chan_deep, 8 * mid_local), BF16),
            pltpu.VMEM((nchip, 2, deep_local, dn), F32),
            pltpu.VMEM((nchip, deep_local, dn), F32),
            pltpu.VMEM((nchip, deep_local, dn), F32),
            pltpu.VMEM((nchip, deep_local, dn), F32),
            pltpu.VMEM((wide, deep_local, dn), F32),
            pltpu.VMEM((27 * deep_local, chan_deep), F32),
            pltpu.VMEM((27 * deep_local, chan_deep), BF16),
            pltpu.VMEM((27 * deep_local, chan_deep), BF16),
            pltpu.VMEM((wide, deep_local, dn), F32),
            pltpu.VMEM((wide, deep_local, 8 * mid_local), F32),
            pltpu.VMEM((8 * mid_local, chan_deep), BF16),
            pltpu.VMEM((8 * mid_local, chan_deep), BF16),
            pltpu.VMEM((wide, mid_local, cells), F32),
            pltpu.VMEM((wide, mid_local, cells), F32),
            dma((sends,)), dma((wide,)),
            dma((sends,)), dma((wide,)),
            dma((sends,)), dma((wide,)),
            dma, dma,
            dma((nchip,)), dma((nchip,)),
            dma((wide,)), dma((wide,)),
            dma((groups,)), dma((groups,)),
            dma((wide,)), dma((wide,)),
            dma,
        ],
        compiler_params=pltpu.CompilerParams(
            collective_id=0, has_side_effects=True, vmem_limit_bytes=56 * 1024 * 1024),
    )(
        mid_input,
        w_conv_mid.reshape(27 * mid_local, chan_mid),
        w_down_mid.reshape(8 * mid_local, chan_deep),
        w_conv_deep.reshape(27 * deep_local, chan_deep),
        up_blocks,
        sel,
    )
    merged = merged.reshape(chan_mid, cells)
    lifted = lax.dot_general(
        w_up_mid, merged, (((1,), (0,)), ((), ())), precision=high)
    lifted = lifted.reshape(2, 4, chan_fine, cells).transpose(2, 0, 1, 3).reshape(chan_fine * 2, 4 * cells)
    return jnp.dot(lifted, fine_sel.T, precision=high).reshape(chan_fine, 2, YA * ZA)


def solution(mesh):
    wide, groups = mesh.shape["wide"], mesh.shape["groups"]
    return jax.shard_map(
        functools.partial(shards, wide, groups),
        mesh=mesh,
        in_specs=(
            P(None, ("groups", "wide"), None),
            P(),
            P(None, "wide", None),
            P(None, "wide", None),
            P(None, "wide", None),
            P(None, "wide", None),
            P(),
        ),
        out_specs=P(None, ("groups", "wide"), None),
        check_vma=False,
    )
```

time: 363 us -> 138 us (0.38); the launches traced: 358 us -> 137 us
  waiting for transfers between devices: 227 us -> 0 us
  Pallas kernels: 0 us -> 115 us
  matrix products: 73.8 us -> 11 us
  other arithmetic: 15.5 us -> 0.94 us
  between operations: 14.3 us -> 0.09 us
  local copies, waits for them, and re-layouts: 23.3 us -> 9.97 us
  starting transfers between devices: 4.33 us -> 0 us
    all_gather x4 -> x0, waiting for transfers between devices: 171 us -> none  [the longest x1 53.2 us: shards(): shard_piece = lax.all_gather(mid_input, 'wide', axis=1, tiled=True)]
    pallas_call x0 -> x1, Pallas kernels: none -> 115 us  [shards(): pl.pallas_call(functools.partial(middle_kernel, wide, groups), out_shape=...]
    dot_general x31 -> x4, matrix products: 71.5 us -> 11 us  [the longest x1 6.46 us: shards(): lax.dot_general(w_down_fine.reshape(8 * chan_fine, chan_mid), picks, (((0...]
    reduce_scatter x1 -> x0, waiting for transfers between devices: 56 us -> none  [shards(): lax.psum_scatter(jnp.einsum('tco,tcn->on', w_down_mid, deep_stack, precis...]
    unnamed x8 -> x0, other arithmetic: 8.85 us -> none
    all_gather x1 -> x0, local copies, waits for them, and re-layouts: 5.63 us -> none  [shards(): shard_piece = lax.all_gather(mid_input, 'wide', axis=1, tiled=True)]
    all_to_all x3 -> x0, local copies, waits for them, and re-layouts: 5.07 us -> none  [shards(): lax.all_to_all(w_up_deep, 'wide', split_axis=2, concat_axis=1, tiled=True)]
    unnamed x32 -> x5, local copies, waits for them, and re-layouts: 6.49 us -> 1.96 us
  transfers between devices with their start and end apart: 6 -> 0, of which waited for: 5 -> 0; matrix products, arithmetic and copies ran while one was open for 12% -> 0% of each run, Pallas kernels for 0% -> 0%
where the time goes in v1:
time: 138 us; the launch traced here: 137 us
  Pallas kernels  115 us (83%)
  matrix products  11 us (8%)
  local copies, waits for them, and re-layouts  9.97 us (7%)
    pallas_call x1, Pallas kernels, shards(): pl.pallas_call(functools.partial(middle_kernel, wide, groups), out_shape=...  115 us
    dot_general x1, matrix products, shards(): lax.dot_general(w_down_fine.reshape(8 * chan_fine, chan_mid), picks, (((0...  6.46 us

profile of v1, /device:TPU:0, one launch (start us, length us, event | category | flops | bytes accessed | tf_op | source)
XLA Modules:
  0.0 136.9 jit_solution(4594402549196859087)
XLA Ops:
  0.0 1.9 %reshape.340 = f32[512,512]{1,0:T(8,128)S(1)} reshape(f32[256,2,512]{2,1,0:T(2,128)} %param.7) | data formatting | bytes 2097152 | tf_op jit(solution)/shard_map/reshape | solution.py:355
  2.0 0.9 convolution_bitcast_fusion
  2.9 0.3 copy.13
  3.2 0.4 reshape.341
  3.6 0.0 copy-start.1
  3.6 0.2 copy.14
  3.8 6.5 %convolution_bitcast_fusion.1.mid_in = f32[512,128]{1,0:T(8,128)} fusion(f32[2048,128]{1,0:T(8,128)S(1)} %bitcast.39, f32[2048,512]{1,0:T(8,128)} %bitcast.36), kind=kOutput, calls=%fused_computation.1 | convolution fusion | flops 805306368 | bytes 5505024 | tf_op jit(solution)/shard_map/dot_general | solution.py:357
  10.3 0.0 copy-done.1
  10.3 2.0 %copy.16 = f32[8,64,512]{1,2,0:T(8,128)} copy(f32[8,64,512]{2,1,0:T(8,128)S(1)} %copy-done.1) | data formatting | bytes 2097152 | tf_op args[5]
  12.2 1.8 %copy.17 = f32[16,64,8,32]{1,3,2,0:T(8,128)S(1)} copy(f32[16,64,8,32]{1,3,0,2:T(8,128)} %bitcast.34) | data formatting | bytes 2097152 | tf_op jit(solution)/shard_map/transpose | solution.py:359
  14.1 1.6 %copy.18.w_up = f32[16,64,256]{2,1,0:T(8,128)} copy(f32[16,64,256]{1,2,0:T(8,128)S(1)} %bitcast.33) | data formatting | bytes 2097152 | tf_op jit(solution)/shard_map/reshape | solution.py:360
  15.6 0.9 convert_convert_fusion.sel
  16.6 0.0 copy-start
  16.6 115.0 %shard_map.73 = f32[16,32,128]{2,1,0:T(8,128)} custom-call(f32[512,128]{1,0:T(8,128)} %convolution_bitcast_fusion.1.mid_in, f32[864,512]{1,0:T(8,128)} %bitcast.40, f32[256,1024]{1,0:T(8,128)} %bitcast.41, f32[1728,1024]{1,0:T(8,128)} %bitcast.35, f32[16,64,256]{2,1,0:T(8,128)} %copy.18.w_up, bf16[512,512]{1,0:T(8,128)(2,1)} %convert_convert_fusion.sel), custom_call_target="tpu_custom_call" | custom-call | tf_op jit(solution)/shard_map/pallas_call | solution.py:366
  131.5 0.0 copy-done
  131.5 2.2 %fusion.43 = f32[128,8,256]{2,0,1:T(8,128)S(1)} fusion(f32[512,128,1]{1,0,2:T(8,128)} %bitcast.42, f32[8,512,256]{2,1,0:T(8,128)S(1)} %copy-done), kind=kOutput, calls=%fused_computation.74 | convolution fusion | flops 805306368 | bytes 5505024 | tf_op jit(solution)/shard_map/dot_general | solution.py:416
  133.8 1.3 fusion.2
  135.1 1.8 %copy.21 = f32[256,2,512]{2,1,0:T(2,128)} copy(f32[256,2,512]{2,0,1:T(8,128)S(1)} %fusion.2) | data formatting | bytes 2097152 | tf_op jit(solution)/shard_map/dot_general | solution.py:419
  (2 shorter events, 0.0 us)
Async XLA Ops:
  3.6 6.7 %copy-start.1 = (f32[8,64,512]{2,1,0:T(8,128)S(1)}, f32[8,64,512]{2,1,0:T(8,128)}, u32[]{:S(2)}) copy-start(f32[8,64,512]{2,1,0:T(8,128)} %param.12) | copy-start | bytes 3145732
  16.6 115.0 %copy-start = (f32[8,512,256]{2,1,0:T(8,128)S(1)}, f32[8,512,256]{2,1,0:T(8,128)}, u32[]{:S(2)}) copy-start(f32[8,512,256]{2,1,0:T(8,128)} %param.13) | copy-start | bytes 12582916

commit v2 on v1

--- a/solution.py
+++ b/solution.py
@@ -2,6 +2,7 @@
 
 import jax
 import jax.numpy as jnp
+import numpy as np
 from jax import lax
 from jax.experimental import pallas as pl
 from jax.experimental.pallas import tpu as pltpu
@@ -17,14 +18,14 @@
 def selector(rows, cols, copies):
     cells = rows * cols
     small = cells // 4
-    source = jnp.arange(copies * cells)[:, None]
-    target = jnp.arange(4 * copies * small)[None, :]
+    source = np.arange(copies * cells)[:, None]
+    target = np.arange(4 * copies * small)[None, :]
     tap = target // (copies * small)
     copy = target // small % copies
     place = target % small
     row = 2 * (place // (cols // 2)) + tap // 2
     col = 2 * (place % (cols // 2)) + tap % 2
-    return (source == copy * cells + row * cols + col).astype(F32)
+    return (source == copy * cells + row * cols + col).astype(np.float32)
 
 
 def split(value):
@@ -46,10 +47,10 @@
 
 def middle_kernel(
     wide, groups,
-    mid_in, w_mid, w_down, w_deep_hbm, w_up, sel, out,
-    xbuf, xh, xl, wmh, wml, acc, mf, wdh, wdl, part, sib, rs, rsin,
+    fine, w_fine_hbm, w_mid_hbm, w_down_hbm, w_deep_hbm, w_up_hbm, w_last_hbm, sel, fsel, out,
+    w_fine, w_mid, w_down, w_up_all, w_last, w_up, wfh, wfl, wlh, wll, pacc, xbuf, xh, xl, wmh, wml, acc, mf, wdh, wdl, part, sib, rs, rsin,
     deep_in, wdeep, wch, wcl, deep_out, wup, wuh, wul, mm, landed,
-    s1, r1, s2, r2, s3, r3, s_sib, r_sib, s_rs, r_rs, s_up, r_up, s_fw, r_fw, s_aa, r_aa, load_sem,
+    s1, r1, s2, r2, s3, r3, s_sib, r_sib, s_rs, r_rs, s_up, r_up, s_fw, r_fw, s_aa, r_aa, load_sems,
 ):
     ny = 2 if wide % 4 == 0 else 1
     nchip = wide // 2
@@ -61,6 +62,7 @@
     y = chip % ny
     z = chip // ny
     mid_local = mf.shape[1]
+    chan_mid = xbuf.shape[1]
     cells = mf.shape[2]
     rows, cols = YA // 2, ZA // 2
     drows, dcols = YA // 4, ZA // 4
@@ -69,8 +71,17 @@
     dn = deep_in.shape[2]
     ngr = dn // cells
 
-    load = pltpu.make_async_copy(w_deep_hbm, wdeep, load_sem)
-    load.start()
+    third = wdeep.shape[1]
+
+    def deep_load(k):
+        return pltpu.make_async_copy(w_deep_hbm.at[pl.ds(k * third, third)], wdeep.at[k % 2], load_sems.at[5 + k])
+
+    sources = (w_up_hbm, w_fine_hbm, w_mid_hbm, w_down_hbm, w_last_hbm)
+    places = (w_up_all, w_fine, w_mid, w_down, w_last)
+    loads = [pltpu.make_async_copy(a, b, load_sems.at[k]) for k, (a, b) in enumerate(zip(sources, places))]
+    load_up, load_fine, load_mid, load_down, load_last = loads
+    for load in loads + [deep_load(0), deep_load(1)]:
+        load.start()
 
     barrier = pltpu.get_barrier_semaphore()
     for step in range(1, wide):
@@ -143,7 +154,47 @@
 
         return finish
 
-    xbuf[me] = mid_in[...]
+    share = wup.shape[1] // groups
+    mine = pl.ds(pl.multiple_of(mygroup * share, share), share)
+
+    def up_move(target, source):
+        return pltpu.make_async_remote_copy(
+            src_ref=w_up.at[target], dst_ref=wup.at[me, mine], send_sem=s_up.at[target], recv_sem=r_up.at[source],
+            device_id={"wide": target}, device_id_type=MESH)
+
+    def up_arrived(source):
+        pltpu.make_async_remote_copy(
+            src_ref=w_up.at[source], dst_ref=wup.at[source, mine], send_sem=s_up.at[source], recv_sem=r_up.at[source],
+            device_id={"wide": source}, device_id_type=MESH).wait_recv()
+
+    load_up.wait()
+    pieces = [w_up_all[t, mine, :] for t in range(8)]
+    for d in range(wide):
+        w_up[d] = jnp.concatenate([piece[:, d * mid_local:(d + 1) * mid_local] for piece in pieces], axis=1)
+    for step in range(1, wide):
+        up_move((me + step) % wide, me).start()
+    wup[me, mine] = w_up[me]
+
+    chan_fine = fine.shape[0]
+    picked_high, picked_low = [], []
+    for a in range(2):
+        high, low = split(fine[:, a, :])
+        high, low = dot_nt(fsel[...], high).astype(BF16), dot_nt(fsel[...], low).astype(BF16)
+        for bc in range(4):
+            picked_high.append(high[bc * cells:(bc + 1) * cells])
+            picked_low.append(low[bc * cells:(bc + 1) * cells])
+    picked_high = jnp.concatenate(picked_high, axis=1)
+    picked_low = jnp.concatenate(picked_low, axis=1)
+    load_fine.wait()
+
+    def split_fine(t, carry):
+        here = pl.ds(pl.multiple_of(t * chan_fine, chan_fine), chan_fine)
+        wfh[here, :], wfl[here, :] = split(w_fine[here, :])
+        return carry
+
+    lax.fori_loop(0, 8, split_fine, 0)
+    both = dot(jnp.concatenate([picked_high, picked_low], axis=0), wfh[...])
+    xbuf[me] = (both[:cells] + both[cells:] + dot(picked_high, wfl[...])).T
     taps = 9 * mid_local
     lane = lax.broadcasted_iota(jnp.int32, (mid_local, cells), 1)
     mid_masks = {}
@@ -179,23 +230,12 @@
 
     def prepare_mid():
         acc[...] = jnp.zeros_like(acc)
+        load_mid.wait()
+        load_down.wait()
         wmh[...], wml[...] = split(w_mid[...])
         wdh[...], wdl[...] = split(w_down[...].T)
 
     finish_mid = gather(xbuf, s1, r1, convolve_mid, prepare_mid)
-
-    share = wup.shape[1] // groups
-    mine = pl.ds(pl.multiple_of(mygroup * share, share), share)
-
-    def up_move(target, source):
-        return pltpu.make_async_remote_copy(
-            src_ref=w_up.at[target, mine], dst_ref=wup.at[me, mine], send_sem=s_up.at[target], recv_sem=r_up.at[source],
-            device_id={"wide": target}, device_id_type=MESH)
-
-    def up_arrived(source):
-        pltpu.make_async_remote_copy(
-            src_ref=w_up.at[source, mine], dst_ref=wup.at[source, mine], send_sem=s_up.at[source], recv_sem=r_up.at[source],
-            device_id={"wide": source}, device_id_type=MESH).wait_recv()
 
     mf[...] = jnp.maximum(acc[1:wide + 1], 0.0)
 
@@ -223,12 +263,14 @@
         device_id={"wide": sibling_id}, device_id_type=MESH)
     pair.start()
 
-    load.wait()
-
-    def split_deep(t, carry):
-        here = pl.ds(pl.multiple_of(t * deep_local, deep_local), deep_local)
-        wch[here, :], wcl[here, :] = split(wdeep[here, :])
-        return carry
+    def split_deep(k):
+        def block(t, carry):
+            here = pl.ds(pl.multiple_of(t * deep_local, deep_local), deep_local)
+            there = pl.ds(pl.multiple_of(k * third + t * deep_local, deep_local), deep_local)
+            wch[there, :], wcl[there, :] = split(wdeep[k % 2, here, :])
+            return carry
+
+        lax.fori_loop(0, 9, block, 0)
 
     pair.wait_recv()
 
@@ -241,11 +283,13 @@
         target = (chip + step) % nchip
         rs[target] = part[target, core] + sib[target]
         rs_move(target, chip, step).start()
-    for step in range(1, wide):
-        target = (me + step) % wide
-        up_move(target, me).start()
-    wup[me, mine] = w_up[me, mine]
-    lax.fori_loop(0, 27, split_deep, 0)
+    deep_load(0).wait()
+    split_deep(0)
+    deep_load(2).start()
+    deep_load(1).wait()
+    split_deep(1)
+    deep_load(2).wait()
+    split_deep(2)
     total = part[chip, core] + sib[chip]
     for step in range(1, nchip):
         source = (chip + nchip - step) % nchip
@@ -256,28 +300,50 @@
     def nothing(*args):
         return None
 
-    finish_in = gather(deep_in, s2, r2, nothing, nothing)
-    for step in range(1, wide):
-        up_arrived((me + wide - step) % wide)
-
     def forward(target, source):
         return pltpu.make_async_remote_copy(
             src_ref=wup.at[:, mine], dst_ref=wup.at[:, mine], send_sem=s_fw.at[target], recv_sem=r_fw.at[mygroup],
             device_id={"groups": target}, device_id_type=MESH)
 
-    for step in range(1, groups):
-        forward((mygroup + step) % groups, mygroup).start()
-
-    dh, dl = split(deep_in[...].reshape(wide * deep_local, dn))
+    def prepare_deep():
+        for step in range(1, wide):
+            up_arrived((me + wide - step) % wide)
+        for step in range(1, groups):
+            forward((mygroup + step) % groups, mygroup).start()
+        load_last.wait()
+        for t in range(8):
+            here = pl.ds(t * chan_mid, chan_mid)
+            wlh[here, :], wll[here, :] = split(w_last[here, :])
+
+    chip_rows = 2 * deep_local
+    by_chip = chip_rows % 128 == 0
+
+    def convolve_deep(at):
+        high, low = split(deep_in[pl.ds(at * 2, 2)].reshape(chip_rows, dn))
+        lanes = pl.ds(pl.multiple_of(at * chip_rows, chip_rows), chip_rows)
+
+        def plane_tap(a, carry):
+            here = pl.ds(pl.multiple_of(a * 9 * deep_local, 9 * deep_local), 9 * deep_local)
+            pacc[here, :] += dot3(wch[here, lanes], wcl[here, lanes], high, low)
+            return carry
+
+        lax.fori_loop(0, 3, plane_tap, 0)
+
+    if by_chip:
+        pacc[...] = jnp.zeros_like(pacc)
+        finish_in = gather(deep_in, s2, r2, convolve_deep, prepare_deep)
+    else:
+        finish_in = gather(deep_in, s2, r2, nothing, prepare_deep)
+        dh, dl = split(deep_in[...].reshape(wide * deep_local, dn))
+        pacc[...] = dot3(wch[...], wcl[...], dh, dl)
     dlane = lax.broadcasted_iota(jnp.int32, (deep_local, dn), 1)
     total = jnp.zeros((deep_local, dn), F32)
     for a in range(3):
-        here = slice(a * 9 * deep_local, (a + 1) * 9 * deep_local)
-        product = dot3(wch[here, :], wcl[here, :], dh, dl)
         for b in range(3):
             for c in range(3):
                 tap = 3 * b + c
-                piece = product[tap * deep_local:(tap + 1) * deep_local]
+                at = (9 * a + tap) * deep_local
+                piece = pacc[at:at + deep_local, :]
                 offset = (a - 1) * dcells + (b - 1) * dcols + c - 1
                 if offset:
                     piece = pltpu.roll(piece, (-offset) % dn, 1)
@@ -337,7 +403,17 @@
     for step in range(1, wide):
         source = (me + wide - step) % wide
         plane_move(source, source).wait_recv()
-    out[...] = landed[...]
+
+    high, low = split(landed[...].reshape(chan_mid, cells).T)
+    both = jnp.concatenate([high, low], axis=0)
+    for a in range(2):
+        rows_of = []
+        for bc in range(4):
+            here = pl.ds((4 * a + bc) * chan_mid, chan_mid)
+            twice = dot(both, wlh[here, :])
+            rows_of.append(twice[:cells] + twice[cells:] + dot(high, wll[here, :]))
+        last_high, last_low = split(jnp.concatenate(rows_of, axis=0).T)
+        out[:, a, :] = dot(last_high, fsel[...]) + dot(last_low, fsel[...])
 
 
 def shards(wide, groups, fine_field, w_down_fine, w_conv_mid, w_down_mid, w_conv_deep, w_up_deep, w_up_mid):
@@ -349,26 +425,30 @@
     cells = YA // 2 * (ZA // 2)
     dn = wide // 2 * (cells // 4)
     nchip = wide // 2
-    high = lax.Precision.HIGH
-
-    fine_sel = selector(YA, ZA, 1)
-    picks = jnp.dot(fine_field.reshape(chan_fine * 2, YA * ZA), fine_sel, precision=high)
-    picks = picks.reshape(chan_fine, 2, 4, cells).transpose(1, 2, 0, 3).reshape(8 * chan_fine, cells)
-    mid_input = lax.dot_general(
-        w_down_fine.reshape(8 * chan_fine, chan_mid), picks, (((0,), (0,)), ((), ())), precision=high)
-    up_blocks = w_up_deep.reshape(8, deep_local, wide, mid_local).transpose(2, 1, 0, 3)
-    up_blocks = up_blocks.reshape(wide, deep_local, 8 * mid_local)
-    sel = selector(YA // 2, ZA // 2, 4).astype(BF16)
+    fine_sel = jnp.asarray(selector(YA, ZA, 1).T, dtype=BF16)
+    sel = jnp.asarray(selector(YA // 2, ZA // 2, 4), dtype=BF16)
 
     vmem = pl.BlockSpec(memory_space=pltpu.VMEM)
     dma = pltpu.SemaphoreType.DMA
     sends = 4 * nchip
-    merged = pl.pallas_call(
+    anywhere = pl.BlockSpec(memory_space=pl.ANY)
+    return pl.pallas_call(
         functools.partial(middle_kernel, wide, groups),
-        out_shape=jax.ShapeDtypeStruct((wide, mid_local, cells), F32),
-        in_specs=[vmem, vmem, vmem, pl.BlockSpec(memory_space=pl.ANY), vmem, vmem],
+        out_shape=jax.ShapeDtypeStruct(fine_field.shape, F32),
+        in_specs=[vmem] + [anywhere] * 6 + [vmem, vmem],
         out_specs=vmem,
         scratch_shapes=[
+            pltpu.VMEM((8 * chan_fine, chan_mid), F32),
+            pltpu.VMEM((27 * mid_local, chan_mid), F32),
+            pltpu.VMEM((8 * mid_local, chan_deep), F32),
+            pltpu.VMEM((8, deep_local, chan_mid), F32),
+            pltpu.VMEM((8 * chan_mid, chan_fine), F32),
+            pltpu.VMEM((wide, deep_local // groups, 8 * mid_local), F32),
+            pltpu.VMEM((8 * chan_fine, chan_mid), BF16),
+            pltpu.VMEM((8 * chan_fine, chan_mid), BF16),
+            pltpu.VMEM((8 * chan_mid, chan_fine), BF16),
+            pltpu.VMEM((8 * chan_mid, chan_fine), BF16),
+            pltpu.VMEM((27 * deep_local, dn), F32),
             pltpu.VMEM((wide, chan_mid, cells), F32),
             pltpu.VMEM((chan_mid, 2 * cells), BF16),
             pltpu.VMEM((chan_mid, 2 * cells), BF16),
@@ -383,7 +463,7 @@
             pltpu.VMEM((nchip, deep_local, dn), F32),
             pltpu.VMEM((nchip, deep_local, dn), F32),
             pltpu.VMEM((wide, deep_local, dn), F32),
-            pltpu.VMEM((27 * deep_local, chan_deep), F32),
+            pltpu.VMEM((2, 9 * deep_local, chan_deep), F32),
             pltpu.VMEM((27 * deep_local, chan_deep), BF16),
             pltpu.VMEM((27 * deep_local, chan_deep), BF16),
             pltpu.VMEM((wide, deep_local, dn), F32),
@@ -400,23 +480,21 @@
             dma((wide,)), dma((wide,)),
             dma((groups,)), dma((groups,)),
             dma((wide,)), dma((wide,)),
-            dma,
+            dma((8,)),
         ],
         compiler_params=pltpu.CompilerParams(
             collective_id=0, has_side_effects=True, vmem_limit_bytes=56 * 1024 * 1024),
     )(
-        mid_input,
+        fine_field,
+        w_down_fine.reshape(8 * chan_fine, chan_mid),
         w_conv_mid.reshape(27 * mid_local, chan_mid),
         w_down_mid.reshape(8 * mid_local, chan_deep),
         w_conv_deep.reshape(27 * deep_local, chan_deep),
-        up_blocks,
+        w_up_deep,
+        w_up_mid.reshape(8 * chan_mid, chan_fine),
         sel,
+        fine_sel,
     )
-    merged = merged.reshape(chan_mid, cells)
-    lifted = lax.dot_general(
-        w_up_mid, merged, (((1,), (0,)), ((), ())), precision=high)
-    lifted = lifted.reshape(2, 4, chan_fine, cells).transpose(2, 0, 1, 3).reshape(chan_fine * 2, 4 * cells)
-    return jnp.dot(lifted, fine_sel.T, precision=high).reshape(chan_fine, 2, YA * ZA)
 
 
 def solution(mesh):

time: 138 us -> 124 us (0.90)
  matrix products: 11 us -> 0 us
  local copies, waits for them, and re-layouts: 9.97 us -> 2.55 us
  Pallas kernels: 115 us -> 120 us
    dot_general x4 -> x0, matrix products: 11 us -> none  [the longest x1 6.46 us: shards(): lax.dot_general(w_down_fine.reshape(8 * chan_fine, chan_mid), picks, (((0...]
    pallas_call x1, Pallas kernels: 115 us -> 120 us  [shards(): pl.pallas_call(functools.partial(middle_kernel, wide, groups), out_shape=...]
    reshape x3 -> x0, local copies, waits for them, and re-layouts: 3.87 us -> none  [the longest x1 1.95 us: shards(): fine_field.reshape(chan_fine * 2, YA * ZA)]
    dot_general x2 -> x0, local copies, waits for them, and re-layouts: 2.11 us -> none  [the longest x1 1.78 us: shards(): jnp.dot(lifted, fine_sel.T, precision=high).reshape(chan_fine, 2, YA * ZA)]
    transpose x2 -> x0, local copies, waits for them, and re-layouts: 2.03 us -> none  [the longest x1 1.82 us: shards(): w_up_deep.reshape(8, deep_local, wide, mid_local).transpose(2, 1, 0, 3)]
where the time goes in v2:
time: 124 us; the launch traced here: 122 us
  Pallas kernels  120 us (97%)
  local copies, waits for them, and re-layouts  2.55 us (2%)
    pallas_call x1, Pallas kernels, shards(): pl.pallas_call(functools.partial(middle_kernel, wide, groups), out_shape=...  120 us
    unnamed x1, local copies, waits for them, and re-layouts  2.55 us

profile of v2, /device:TPU:0, one launch (start us, length us, event | category | flops | bytes accessed | tf_op | source)
XLA Modules:
  0.0 122.3 jit_solution(2597700235271858799)
XLA Ops:
  0.0 119.7 %shard_map.91 = f32[256,2,512]{2,1,0:T(2,128)} custom-call(f32[256,2,512]{2,1,0:T(2,128)} %fine.1, f32[2048,512]{1,0:T(8,128)} %bitcast.6, f32[864,512]{1,0:T(8,128)} %bitcast.8, f32[256,1024]{1,0:T(8,128)} %bitcast.9, f32[1728,1024]{1,0:T(8,128)} %bitcast.5, f32[8,64,512]{2,1,0:T(8,128)} %w_up_hbm.1, f32[4096,256]{1,0:T(8,128)} %bitcast.7, ...), custom_call_target="tpu_custom_call" | custom-call | tf_op jit(solution)/shard_map/pallas_call | solution.py:435
  119.7 2.6 %copy.11 = f32[256,2,512]{2,1,0:T(2,128)} copy(f32[256,2,512]{2,1,0:T(2,128)} %shard_map.91) | data formatting | bytes 2097152

commit v3 on v2

--- a/solution.py
+++ b/solution.py
@@ -93,46 +93,57 @@
     def slot(zz, yy, cc):
         return (zz * ny + yy) * 2 + cc
 
-    def gather(buf, send_sem, recv_sem, consume, idle):
-        def move(at, target, k):
+    def gather(buf, send_sem, recv_sem, parts, consume, idle):
+        piece = buf.shape[1] // parts
+
+        def move(at, target, k, part):
+            here = buf.at[at, pl.ds(part * piece, piece)]
             return pltpu.make_async_remote_copy(
-                src_ref=buf.at[at], dst_ref=buf.at[at], send_sem=send_sem.at[k], recv_sem=recv_sem.at[at],
+                src_ref=here, dst_ref=here, send_sem=send_sem.at[k, part], recv_sem=recv_sem.at[at, part],
                 device_id={"wide": target}, device_id_type=MESH)
 
-        def arrived(at):
-            move(at, slot(z, y, 1 - core), 0).wait_recv()
+        def arrived(at, part):
+            move(at, slot(z, y, 1 - core), 0, part).wait_recv()
+
+        def all_arrived(at):
+            for part in range(parts):
+                arrived(at, part)
 
         sibling = slot(z, y, 1 - core)
         other = slot(z, ny - 1 - y, core)
-        if ny == 2:
-            move(me, other, nz).start()
-        move(me, sibling, 2 * nz).start()
+        for part in range(parts):
+            if ny == 2:
+                move(me, other, nz, part).start()
+            move(me, sibling, 2 * nz, part).start()
         for dz in range(1, nz):
-            move(me, slot((z + nz - dz) % nz, y, core), dz - 1).start()
+            for part in range(parts):
+                move(me, slot((z + nz - dz) % nz, y, core), dz - 1, part).start()
         idle()
-        arrived(sibling)
+        all_arrived(sibling)
         consume(chip)
 
         def other_row(dz):
             zp = (z + dz) % nz
             at = slot(zp, 1 - y, core)
-            arrived(at)
-            move(at, sibling, 2 * nz + dz * ny + 1).start()
+            for part in range(parts):
+                arrived(at, part)
+                move(at, sibling, 2 * nz + dz * ny + 1, part).start()
 
         def step(dz, carry):
             zs = (z + dz) % nz
             at = slot(zs, y, core)
-            arrived(at)
-            if ny == 2:
-                move(at, other, nz + dz).start()
-            move(at, sibling, 2 * nz + dz * ny).start()
+            for part in range(parts):
+                arrived(at, part)
+                if ny == 2:
+                    move(at, other, nz + dz, part).start()
+                move(at, sibling, 2 * nz + dz * ny, part).start()
             if ny == 2:
                 other_row(dz - 1)
-            arrived(slot(zs, y, 1 - core))
+            all_arrived(slot(zs, y, 1 - core))
             consume(zs * ny + y)
             if ny == 2:
                 zp = (z + dz - 1) % nz
-                arrived(slot(zp, 1 - y, 1 - core))
+                all_arrived(slot(zp, 1 - y, 1 - core))
                 consume(zp * ny + 1 - y)
             return carry
 
@@ -140,17 +151,16 @@
         if ny == 2:
             other_row(nz - 1)
             zp = (z + nz - 1) % nz
-            arrived(slot(zp, 1 - y, 1 - core))
+            all_arrived(slot(zp, 1 - y, 1 - core))
             consume(zp * ny + 1 - y)
 
         def finish():
-            for k in range(nz - 1):
-                move(me, sibling, k).wait_send()
+            keys = list(range(nz - 1)) + list(range(2 * nz, 2 * nz + nz * ny))
             if ny == 2:
-                for k in range(nz):
-                    move(me, sibling, nz + k).wait_send()
-            for k in range(nz * ny):
-                move(me, sibling, 2 * nz + k).wait_send()
+                keys += list(range(nz, 2 * nz))
+            for k in keys:
+                for part in range(parts):
+                    move(me, sibling, k, part).wait_send()
 
         return finish
 
@@ -235,7 +245,7 @@
         wmh[...], wml[...] = split(w_mid[...])
         wdh[...], wdl[...] = split(w_down[...].T)
 
-    finish_mid = gather(xbuf, s1, r1, convolve_mid, prepare_mid)
+    finish_mid = gather(xbuf, s1, r1, 2, convolve_mid, prepare_mid)
 
     mf[...] = jnp.maximum(acc[1:wide + 1], 0.0)
 
@@ -283,6 +293,15 @@
         target = (chip + step) % nchip
         rs[target] = part[target, core] + sib[target]
         rs_move(target, chip, step).start()
+    def forward(target, source):
+        return pltpu.make_async_remote_copy(
+            src_ref=wup.at[:, mine], dst_ref=wup.at[:, mine], send_sem=s_fw.at[target], recv_sem=r_fw.at[mygroup],
+            device_id={"groups": target}, device_id_type=MESH)
+
+    for step in range(1, wide):
+        up_arrived((me + wide - step) % wide)
+    for step in range(1, groups):
+        forward((mygroup + step) % groups, mygroup).start()
     deep_load(0).wait()
     split_deep(0)
     deep_load(2).start()
@@ -290,6 +309,14 @@
     split_deep(1)
     deep_load(2).wait()
     split_deep(2)
+    load_last.wait()
+
+    def split_last(t, carry):
+        here = pl.ds(pl.multiple_of(t * chan_mid, chan_mid), chan_mid)
+        wlh[here, :], wll[here, :] = split(w_last[here, :])
+        return carry
+
+    lax.fori_loop(0, 8, split_last, 0)
     total = part[chip, core] + sib[chip]
     for step in range(1, nchip):
         source = (chip + nchip - step) % nchip
@@ -300,20 +327,14 @@
     def nothing(*args):
         return None
 
-    def forward(target, source):
-        return pltpu.make_async_remote_copy(
-            src_ref=wup.at[:, mine], dst_ref=wup.at[:, mine], send_sem=s_fw.at[target], recv_sem=r_fw.at[mygroup],
-            device_id={"groups": target}, device_id_type=MESH)
-
     def prepare_deep():
-        for step in range(1, wide):
-            up_arrived((me + wide - step) % wide)
         for step in range(1, groups):
-            forward((mygroup + step) % groups, mygroup).start()
-        load_last.wait()
-        for t in range(8):
-            here = pl.ds(t * chan_mid, chan_mid)
-            wlh[here, :], wll[here, :] = split(w_last[here, :])
+            source = (mygroup + groups - step) % groups
+            theirs = pl.ds(pl.multiple_of(source * share, share), share)
+            pltpu.make_async_remote_copy(
+                src_ref=wup.at[:, theirs], dst_ref=wup.at[:, theirs], send_sem=s_fw.at[source],
+                recv_sem=r_fw.at[source], device_id={"groups": source}, device_id_type=MESH).wait_recv()
+        wuh[...], wul[...] = split(wup[...].reshape(wide * deep_local, wup.shape[2]).T)
 
     chip_rows = 2 * deep_local
     by_chip = chip_rows % 128 == 0
@@ -331,9 +352,9 @@
 
     if by_chip:
         pacc[...] = jnp.zeros_like(pacc)
-        finish_in = gather(deep_in, s2, r2, convolve_deep, prepare_deep)
+        finish_in = gather(deep_in, s2, r2, 1, convolve_deep, prepare_deep)
     else:
-        finish_in = gather(deep_in, s2, r2, nothing, prepare_deep)
+        finish_in = gather(deep_in, s2, r2, 1, nothing, prepare_deep)
         dh, dl = split(deep_in[...].reshape(wide * deep_local, dn))
         pacc[...] = dot3(wch[...], wcl[...], dh, dl)
     dlane = lax.broadcasted_iota(jnp.int32, (deep_local, dn), 1)
@@ -353,16 +374,7 @@
                 total = total + piece
     deep_out[me] = jnp.maximum(total, 0.0)
 
-    def prepare_up():
-        for step in range(1, groups):
-            source = (mygroup + groups - step) % groups
-            theirs = pl.ds(pl.multiple_of(source * share, share), share)
-            pltpu.make_async_remote_copy(
-                src_ref=wup.at[:, theirs], dst_ref=wup.at[:, theirs], send_sem=s_fw.at[source],
-                recv_sem=r_fw.at[source], device_id={"groups": source}, device_id_type=MESH).wait_recv()
-        wuh[...], wul[...] = split(wup[...].reshape(wide * deep_local, wup.shape[2]).T)
-
-    finish_out = gather(deep_out, s3, r3, nothing, prepare_up)
+    finish_out = gather(deep_out, s3, r3, 1, nothing, nothing)
     dh, dl = split(deep_out[...].reshape(wide * deep_local, dn))
     lifted = dot3(wuh[...], wul[...], dh, dl)
     blocks = []
@@ -413,7 +425,7 @@
             twice = dot(both, wlh[here, :])
             rows_of.append(twice[:cells] + twice[cells:] + dot(high, wll[here, :]))
         last_high, last_low = split(jnp.concatenate(rows_of, axis=0).T)
-        out[:, a, :] = dot(last_high, fsel[...]) + dot(last_low, fsel[...])
+        out[a] = dot(last_high, fsel[...]) + dot(last_low, fsel[...])
 
 
 def shards(wide, groups, fine_field, w_down_fine, w_conv_mid, w_down_mid, w_conv_deep, w_up_deep, w_up_mid):
@@ -432,9 +444,9 @@
     dma = pltpu.SemaphoreType.DMA
     sends = 4 * nchip
     anywhere = pl.BlockSpec(memory_space=pl.ANY)
-    return pl.pallas_call(
+    turned = pl.pallas_call(
         functools.partial(middle_kernel, wide, groups),
-        out_shape=jax.ShapeDtypeStruct(fine_field.shape, F32),
+        out_shape=jax.ShapeDtypeStruct((2, chan_fine, YA * ZA), F32),
         in_specs=[vmem] + [anywhere] * 6 + [vmem, vmem],
         out_specs=vmem,
         scratch_shapes=[
@@ -472,9 +484,9 @@
             pltpu.VMEM((8 * mid_local, chan_deep), BF16),
             pltpu.VMEM((wide, mid_local, cells), F32),
             pltpu.VMEM((wide, mid_local, cells), F32),
-            dma((sends,)), dma((wide,)),
-            dma((sends,)), dma((wide,)),
-            dma((sends,)), dma((wide,)),
+            dma((sends, 2)), dma((wide, 2)),
+            dma((sends, 1)), dma((wide, 1)),
+            dma((sends, 1)), dma((wide, 1)),
             dma, dma,
             dma((nchip,)), dma((nchip,)),
             dma((wide,)), dma((wide,)),
@@ -495,6 +507,7 @@
         sel,
         fine_sel,
     )
+    return turned.transpose(1, 0, 2)
 
 
 def solution(mesh):

time: 124 us -> 123 us (level)
    transpose x0 -> x1, local copies, waits for them, and re-layouts: none -> 3 us  [shards(): return turned.transpose(1, 0, 2)]
    unnamed x1 -> x0, local copies, waits for them, and re-layouts: 2.55 us -> none
where the time goes in v3:
time: 123 us; the launch traced here: 122 us
  Pallas kernels  119 us (97%)
  local copies, waits for them, and re-layouts  3 us (2%)
    pallas_call x1, Pallas kernels, shards(): pl.pallas_call(functools.partial(middle_kernel, wide, groups), out_shape=...  119 us
    transpose x1, local copies, waits for them, and re-layouts, shards(): return turned.transpose(1, 0, 2)  3 us

profile of v3, /device:TPU:0, one launch (start us, length us, event | category | flops | bytes accessed | tf_op | source)
XLA Modules:
  0.0 121.5 jit_solution(7013974841892710270)
XLA Ops:
  0.0 118.5 %shard_map.91 = f32[2,256,512]{2,1,0:T(8,128)} custom-call(f32[256,2,512]{2,1,0:T(2,128)} %fine.1, f32[2048,512]{1,0:T(8,128)} %bitcast.8, f32[864,512]{1,0:T(8,128)} %bitcast.10, f32[256,1024]{1,0:T(8,128)} %bitcast.11, f32[1728,1024]{1,0:T(8,128)} %bitcast.6, f32[8,64,512]{2,1,0:T(8,128)} %w_up_hbm.1, f32[4096,256]{1,0:T(8,128)} %bitcast.9, ...), custom_call_target="tpu_custom_call" | custom-call | tf_op jit(solution)/shard_map/pallas_call | solution.py:447
  118.5 3.0 %copy.10 = f32[256,2,512]{2,1,0:T(2,128)} copy(f32[256,2,512]{2,0,1:T(8,128)} %bitcast.7) | data formatting | bytes 2097152 | tf_op jit(solution)/shard_map/transpose | solution.py:510

commit v4 on v3

--- a/solution.py
+++ b/solution.py
@@ -181,8 +181,6 @@
     pieces = [w_up_all[t, mine, :] for t in range(8)]
     for d in range(wide):
         w_up[d] = jnp.concatenate([piece[:, d * mid_local:(d + 1) * mid_local] for piece in pieces], axis=1)
-    for step in range(1, wide):
-        up_move((me + step) % wide, me).start()
     wup[me, mine] = w_up[me]
 
     chan_fine = fine.shape[0]
@@ -247,6 +245,8 @@
 
     finish_mid = gather(xbuf, s1, r1, 2, convolve_mid, prepare_mid)
 
+    for step in range(1, wide):
+        up_move((me + step) % wide, me).start()
     mf[...] = jnp.maximum(acc[1:wide + 1], 0.0)
 
     gathered = []
@@ -298,10 +298,6 @@
             src_ref=wup.at[:, mine], dst_ref=wup.at[:, mine], send_sem=s_fw.at[target], recv_sem=r_fw.at[mygroup],
             device_id={"groups": target}, device_id_type=MESH)
 
-    for step in range(1, wide):
-        up_arrived((me + wide - step) % wide)
-    for step in range(1, groups):
-        forward((mygroup + step) % groups, mygroup).start()
     deep_load(0).wait()
     split_deep(0)
     deep_load(2).start()
@@ -328,13 +324,10 @@
         return None
 
     def prepare_deep():
+        for step in range(1, wide):
+            up_arrived((me + wide - step) % wide)
         for step in range(1, groups):
-            source = (mygroup + groups - step) % groups
-            theirs = pl.ds(pl.multiple_of(source * share, share), share)
-            pltpu.make_async_remote_copy(
-                src_ref=wup.at[:, theirs], dst_ref=wup.at[:, theirs], send_sem=s_fw.at[source],
-                recv_sem=r_fw.at[source], device_id={"groups": source}, device_id_type=MESH).wait_recv()
-        wuh[...], wul[...] = split(wup[...].reshape(wide * deep_local, wup.shape[2]).T)
+            forward((mygroup + step) % groups, mygroup).start()
 
     chip_rows = 2 * deep_local
     by_chip = chip_rows % 128 == 0
@@ -374,7 +367,16 @@
                 total = total + piece
     deep_out[me] = jnp.maximum(total, 0.0)
 
-    finish_out = gather(deep_out, s3, r3, 1, nothing, nothing)
+    def prepare_up():
+        for step in range(1, groups):
+            source = (mygroup + groups - step) % groups
+            theirs = pl.ds(pl.multiple_of(source * share, share), share)
+            pltpu.make_async_remote_copy(
+                src_ref=wup.at[:, theirs], dst_ref=wup.at[:, theirs], send_sem=s_fw.at[source],
+                recv_sem=r_fw.at[source], device_id={"groups": source}, device_id_type=MESH).wait_recv()
+        wuh[...], wul[...] = split(wup[...].reshape(wide * deep_local, wup.shape[2]).T)
+
+    finish_out = gather(deep_out, s3, r3, 1, nothing, prepare_up)
     dh, dl = split(deep_out[...].reshape(wide * deep_local, dn))
     lifted = dot3(wuh[...], wul[...], dh, dl)
     blocks = []

time: 123 us -> 126 us (1.024)
  Pallas kernels: 119 us -> 121 us
    pallas_call x1, Pallas kernels: 119 us -> 121 us  [shards(): pl.pallas_call(functools.partial(middle_kernel, wide, groups), out_shape=...]
where the time goes in v4:
time: 126 us; the launch traced here: 124 us
  Pallas kernels  121 us (96%)
  local copies, waits for them, and re-layouts  3 us (2%)
    pallas_call x1, Pallas kernels, shards(): pl.pallas_call(functools.partial(middle_kernel, wide, groups), out_shape=...  121 us
    transpose x1, local copies, waits for them, and re-layouts, shards(): return turned.transpose(1, 0, 2)  3 us

profile of v4, /device:TPU:0, one launch (start us, length us, event | category | flops | bytes accessed | tf_op | source)
XLA Modules:
  0.0 124.3 jit_solution(8349209258790634300)
XLA Ops:
  0.0 121.2 %shard_map.91 = f32[2,256,512]{2,1,0:T(8,128)} custom-call(f32[256,2,512]{2,1,0:T(2,128)} %fine.1, f32[2048,512]{1,0:T(8,128)} %bitcast.8, f32[864,512]{1,0:T(8,128)} %bitcast.10, f32[256,1024]{1,0:T(8,128)} %bitcast.11, f32[1728,1024]{1,0:T(8,128)} %bitcast.6, f32[8,64,512]{2,1,0:T(8,128)} %w_up_hbm.1, f32[4096,256]{1,0:T(8,128)} %bitcast.9, ...), custom_call_target="tpu_custom_call" | custom-call | tf_op jit(solution)/shard_map/pallas_call | solution.py:449
  121.3 3.0 %copy.10 = f32[256,2,512]{2,1,0:T(2,128)} copy(f32[256,2,512]{2,0,1:T(8,128)} %bitcast.7) | data formatting | bytes 2097152 | tf_op jit(solution)/shard_map/transpose | solution.py:512
